TPU v7x, 32 devices: a whole 2x2x4 slice. The times are simulated.
32 devices in a mesh: dp: 16 (over z, y, x), owner: 2 (over core).
Axes of the slice: x: 2, y: 2, z: 4, core: 2. Of those that a mesh axis runs over, the one named last changes fastest.
Arguments:
- query_out: bfloat16 [128, 4096], P('dp', 'owner'), may hold values from -6 to 6
- query_in: bfloat16 [128, 8192], P('dp'), may hold values from -6 to 6
- train_out: bfloat16 [128, 4096], P('dp', 'owner'), may hold values from -6 to 6
- train_in: bfloat16 [128, 8192], P('dp'), may hold values from -6 to 6
- basis_out: bfloat16 [24, 256, 256], P('owner'), may hold values from -1 to 1, as said below
- basis_in: bfloat16 [64, 128, 128], P('dp'), may hold values from -1 to 1, as said below
- eigvals: float32 [6144, 8192], P('owner', 'dp'), may hold values from 0.1 to 10
- owner_map: int32 [16], replicated, may hold values from 0 to 1, as said below
Outputs:
- scores: float32 [8, 8], replicated
Inputs may be any that keep to these rules, and one draw needn't show every extreme that they name: owner_map[b] is the owner of hidden block b. Blocks form ranges of 8 in order; a block of range r is owned by r or by r xor 1. Of two such partner owners one holds exactly 12 blocks and keeps 12 // 2 of its own range, the other holds 4 blocks and keeps 8 - 12 // 2 of its own range. `basis_out`: each [256, 256] block is an orthogonal matrix rounded to bfloat16; block o * 12 + s belongs to the s-th block, in block order, that owner o holds; blocks past an owner's count are not read. `basis_in`: each [128, 128] block is an orthogonal matrix rounded to bfloat16.
All inputs are finite; a program needn't handle non-finite values.
Results may differ from a plain program's by a relative error of at most 0.0067.
Values may be sent and summed in bfloat16 or wider, within the bound.
A program may use at most 128 MiB of HBM per device.

v0:
```python
import math

import jax
import jax.numpy as jnp
from jax import lax
from jax.sharding import PartitionSpec as P

NQ = 8
ET = 16


DAMPING = 0.1


def from_partner(array, axis, stride):
    return lax.ppermute(array, axis, [(i, i ^ 1 << stride) for i in range(lax.axis_size(axis))])


def slot_tables(owner_map, owner_index, blocks_own, capacity):
    pair_count = 2 * blocks_own
    pair_base = owner_index // 2 * pair_count
    pair_owner = lax.dynamic_slice_in_dim(owner_map, pair_base, pair_count)
    owned_mask = (pair_owner == owner_index).astype(jnp.int32)
    slot_rank = jnp.cumsum(owned_mask) - 1
    slot_ids = jnp.arange(capacity, dtype=jnp.int32)
    pair_hot = (owned_mask[:, None] == 1) & (slot_rank[:, None] == slot_ids[None, :])
    own_start = owner_index % 2 * blocks_own
    other_start = blocks_own - own_start
    keep_hot = lax.dynamic_slice_in_dim(pair_hot, own_start, blocks_own, 0)
    other_hot = lax.dynamic_slice_in_dim(pair_hot, other_start, blocks_own, 0)
    send_ids = jnp.arange(capacity // 2, dtype=jnp.int32)
    from_other = lax.dynamic_slice_in_dim(owned_mask, other_start, blocks_own)
    other_rank = jnp.cumsum(from_other) - 1
    arrive_hot = (from_other[:, None] == 1) & (other_rank[:, None] == send_ids[None, :])
    arrive_slot = jnp.dot(arrive_hot.T.astype(jnp.float32), other_hot.astype(jnp.float32))
    to_other = 1 - lax.dynamic_slice_in_dim(owned_mask, own_start, blocks_own)
    depart_rank = jnp.cumsum(to_other) - 1
    depart_hot = (to_other[:, None] == 1) & (depart_rank[:, None] == send_ids[None, :])
    return (
        keep_hot.astype(jnp.bfloat16),
        depart_hot.astype(jnp.bfloat16),
        arrive_slot.astype(jnp.bfloat16),
    )


def departing(tokens, depart_hot, block_width):
    blocks = tokens.reshape(tokens.shape[0], -1, block_width)
    return jnp.einsum("rpk,ps->rsk", blocks, depart_hot, preferred_element_type=jnp.float32).astype(
        jnp.bfloat16
    )


def to_slots(tokens, arrived, keep_hot, arrive_slot, block_width):
    blocks = tokens.reshape(tokens.shape[0], -1, block_width)
    kept_part = jnp.einsum("rpk,pc->rck", blocks, keep_hot, preferred_element_type=jnp.float32)
    moved_part = jnp.einsum("rsk,sc->rck", arrived, arrive_slot, preferred_element_type=jnp.float32)
    return (kept_part + moved_part).astype(jnp.bfloat16)


def rotate_outputs(slotted, basis_out):
    return jnp.einsum(
        "rck,ckl->rcl", slotted, basis_out, preferred_element_type=jnp.float32
    ).astype(jnp.bfloat16)


def rotate_inputs(columns_local, basis_in):
    token_count = columns_local.shape[0]
    blocks = columns_local.reshape(token_count, basis_in.shape[0], basis_in.shape[1])
    turned = jnp.einsum("tnb,nbc->tnc", blocks, basis_in, preferred_element_type=jnp.float32)
    return turned.astype(jnp.bfloat16).reshape(token_count, -1)


def condition(query_rot, query_act, eigvals, basis_in, basis_out):
    capacity, block_width = (basis_out.shape[0], basis_out.shape[1])
    in_blocks, in_width = (basis_in.shape[0], basis_in.shape[1])
    per_query = query_rot.shape[0] // NQ
    query_flat = query_rot.reshape(query_rot.shape[0], capacity * block_width)
    shifted = eigvals + DAMPING
    results = []
    for query_index in range(NQ):
        left_side = query_flat[query_index * per_query : (query_index + 1) * per_query]
        right_side = query_act[query_index * per_query : (query_index + 1) * per_query]
        moment = lax.dot_general(
            left_side, right_side, (((0,), (0,)), ((), ())), preferred_element_type=jnp.float32
        )
        damped = (moment / shifted).astype(jnp.bfloat16)
        half_back = jnp.einsum(
            "fnb,ncb->fnc",
            damped.reshape(-1, in_blocks, in_width),
            basis_in,
            preferred_element_type=jnp.float32,
        ).astype(jnp.bfloat16)
        restored = jnp.einsum(
            "ckl,cld->ckd",
            basis_out,
            half_back.reshape(capacity, block_width, -1),
            preferred_element_type=jnp.float32,
        ).astype(jnp.bfloat16)
        results.append(restored.reshape(capacity * block_width, -1))
    return jnp.stack(results)


def score_tokens(precond, train_slots, train_inputs, example_count):
    projected = jnp.einsum("tf,qfd->qtd", train_slots, precond, preferred_element_type=jnp.float32)
    per_token = jnp.sum(projected * train_inputs.astype(jnp.float32)[None], axis=2)
    token_ids = jnp.arange(train_slots.shape[0], dtype=jnp.int32)
    example_hot = (
        token_ids[:, None] // ET == jnp.arange(example_count, dtype=jnp.int32)[None, :]
    ).astype(jnp.float32)
    return jnp.dot(per_token, example_hot, precision=lax.Precision.HIGHEST)


def local(query_out, query_in, train_out, train_in, basis_out, basis_in, eigvals, owner_map):
    owner_index = lax.axis_index("owner")
    capacity = basis_out.shape[0]
    block_width = basis_out.shape[1]
    blocks_own = query_out.shape[1] // block_width
    query_local = query_out.shape[0]
    keep_hot, depart_hot, arrive_slot = slot_tables(owner_map, owner_index, blocks_own, capacity)
    query_cols, train_cols = (
        lax.all_to_all(query_in, "dp", split_axis=1, concat_axis=0, tiled=True),
        lax.all_to_all(train_in, "dp", split_axis=1, concat_axis=0, tiled=True),
    )
    query_act = rotate_inputs(query_cols, basis_in)
    example_count = train_cols.shape[0] // ET
    local_tokens = jnp.concatenate([query_out, train_out], 0)
    leaving = departing(local_tokens, depart_hot, block_width)
    arrived = from_partner(leaving, "owner", 0)
    slotted = to_slots(local_tokens, arrived, keep_hot, arrive_slot, block_width)
    query_rot = rotate_outputs(slotted[:query_local], basis_out)
    train_local = slotted[query_local:]
    query_all = lax.all_gather(query_rot, "dp", axis=0, tiled=True)
    precond = condition(query_all, query_act, eigvals, basis_in, basis_out)
    piece_slots = lax.all_gather(train_local, "dp", axis=0, tiled=True)
    row_count = piece_slots.shape[0]
    partial_scores = score_tokens(
        precond, piece_slots.reshape(row_count, -1), train_cols, example_count
    )
    scores = lax.psum(partial_scores, ("dp", "owner"))
    per_query = query_act.shape[0] // NQ
    hidden_total = query_out.shape[1] * lax.axis_size("owner")
    score_scale = 1.0 / math.sqrt(per_query * ET * hidden_total * query_in.shape[1])
    return scores * score_scale


def solution(mesh):
    in_specs = (
        P("dp", "owner"),
        P("dp", None),
        P("dp", "owner"),
        P("dp", None),
        P("owner", None, None),
        P("dp", None, None),
        P("owner", "dp"),
        P(),
    )
    out_specs = P()
    return jax.shard_map(local, mesh=mesh, in_specs=in_specs, out_specs=out_specs, check_vma=False)
```

profile of v0, /device:TPU:0, one launch (start us, length us, event | category | flops | bytes accessed | tf_op | source)
XLA Modules:
  0.0 480.3 jit_solution(1725210853092411357)
XLA Ops:
  2.6 7.9 %all-to-all-start = ((bf16[8,16,512]{2,0,1:T(8,128)(2,1)}), bf16[8,16,512]{2,0,1:T(8,128)(2,1)S(1)}, u32[]{:S(2)}, u32[]{:S(2)}) async-start(bf16[8,16,512]{2,0,1:T(8,128)(2,1)} %bitcast.224), calls=%async_computation | async-start | bytes 262144 | tf_op jit(solution)/shard_map/all_to_all | solution.py:121
  11.7 6.6 %copy.112 = f32[3072,512]{0,1:T(8,128)} copy(f32[3072,512]{1,0:T(8,128)} %param.14) | data formatting | bytes 12582912 | tf_op args[6]
  19.2 45.7 %all_gather.6 = bf16[128,12,256]{2,0,1:T(8,128)(2,1)S(1)} all-gather(bf16[8,12,256]{2,0,1:T(8,128)(2,1)S(1)} %fusion.13), channel_id=1, replica_groups=mesh['dp'=16,'owner'=2] {'dp'}, dimensions={0}, use_global_device_ids=true | all-gather | bytes 835584 | tf_op jit(solution)/shard_map/all_gather | solution.py:132
  69.5 40.5 %all_gather.7 = bf16[128,12,256]{2,0,1:T(8,128)(2,1)S(1)} all-gather(bf16[8,12,256]{2,0,1:T(8,128)(2,1)S(1)} %copy.151), channel_id=1, replica_groups=mesh['dp'=16,'owner'=2] {'dp'}, dimensions={0}, use_global_device_ids=true | all-gather | bytes 835584 | tf_op jit(solution)/shard_map/all_gather | solution.py:134
  120.1 15.6 %copy.114 = bf16[3072,4,128]{2,1,0:T(4,128)(2,1)} copy(bf16[3072,4,128]{2,0,1:T(8,128)(2,1)S(1)} %fusion) | data formatting | bytes 6291456 | tf_op jit(solution)/shard_map/convert_element_type | solution.py:92
  135.7 5.7 %reshape.211 = bf16[12,256,512]{2,1,0:T(8,128)(2,1)} reshape(bf16[3072,4,128]{2,1,0:T(4,128)(2,1)} %copy.114) | data formatting | bytes 6291456 | tf_op jit(solution)/shard_map/reshape | solution.py:96
  146.0 4.8 copy.143
  155.8 15.8 %copy.118 = bf16[3072,4,128]{2,1,0:T(4,128)(2,1)} copy(bf16[3072,4,128]{2,0,1:T(8,128)(2,1)S(1)} %fusion.1) | data formatting | bytes 6291456 | tf_op jit(solution)/shard_map/convert_element_type | solution.py:92
  171.6 5.7 %reshape.213 = bf16[12,256,512]{2,1,0:T(8,128)(2,1)} reshape(bf16[3072,4,128]{2,1,0:T(4,128)(2,1)} %copy.118) | data formatting | bytes 6291456 | tf_op jit(solution)/shard_map/reshape | solution.py:96
  191.6 15.8 %copy.122 = bf16[3072,4,128]{2,1,0:T(4,128)(2,1)} copy(bf16[3072,4,128]{2,0,1:T(8,128)(2,1)S(1)} %fusion.2) | data formatting | bytes 6291456 | tf_op jit(solution)/shard_map/convert_element_type | solution.py:92
  207.4 5.7 %reshape.215 = bf16[12,256,512]{2,1,0:T(8,128)(2,1)} reshape(bf16[3072,4,128]{2,1,0:T(4,128)(2,1)} %copy.122) | data formatting | bytes 6291456 | tf_op jit(solution)/shard_map/reshape | solution.py:96
  227.4 15.9 %copy.126 = bf16[3072,4,128]{2,1,0:T(4,128)(2,1)} copy(bf16[3072,4,128]{2,0,1:T(8,128)(2,1)S(1)} %fusion.3) | data formatting | bytes 6291456 | tf_op jit(solution)/shard_map/convert_element_type | solution.py:92
  243.3 5.7 %reshape.217 = bf16[12,256,512]{2,1,0:T(8,128)(2,1)} reshape(bf16[3072,4,128]{2,1,0:T(4,128)(2,1)} %copy.126) | data formatting | bytes 6291456 | tf_op jit(solution)/shard_map/reshape | solution.py:96
  253.6 4.7 copy.146
  263.3 16.1 %copy.130 = bf16[3072,4,128]{2,1,0:T(4,128)(2,1)} copy(bf16[3072,4,128]{2,0,1:T(8,128)(2,1)S(1)} %fusion.4) | data formatting | bytes 6291456 | tf_op jit(solution)/shard_map/convert_element_type | solution.py:92
  279.4 5.7 %reshape.219 = bf16[12,256,512]{2,1,0:T(8,128)(2,1)} reshape(bf16[3072,4,128]{2,1,0:T(4,128)(2,1)} %copy.130) | data formatting | bytes 6291456 | tf_op jit(solution)/shard_map/reshape | solution.py:96
  299.4 15.8 %copy.134 = bf16[3072,4,128]{2,1,0:T(4,128)(2,1)} copy(bf16[3072,4,128]{2,0,1:T(8,128)(2,1)S(1)} %fusion.5) | data formatting | bytes 6291456 | tf_op jit(solution)/shard_map/convert_element_type | solution.py:92
  315.2 5.7 %reshape.221 = bf16[12,256,512]{2,1,0:T(8,128)(2,1)} reshape(bf16[3072,4,128]{2,1,0:T(4,128)(2,1)} %copy.134) | data formatting | bytes 6291456 | tf_op jit(solution)/shard_map/reshape | solution.py:96
  335.2 15.8 %copy.138 = bf16[3072,4,128]{2,1,0:T(4,128)(2,1)} copy(bf16[3072,4,128]{2,0,1:T(8,128)(2,1)S(1)} %fusion.6) | data formatting | bytes 6291456 | tf_op jit(solution)/shard_map/convert_element_type | solution.py:92
  351.0 5.7 %reshape.223 = bf16[12,256,512]{2,1,0:T(8,128)(2,1)} reshape(bf16[3072,4,128]{2,1,0:T(4,128)(2,1)} %copy.138) | data formatting | bytes 6291456 | tf_op jit(solution)/shard_map/reshape | solution.py:96
  371.0 15.9 %copy.142 = bf16[3072,4,128]{2,1,0:T(4,128)(2,1)} copy(bf16[3072,4,128]{2,0,1:T(8,128)(2,1)S(1)} %fusion.7) | data formatting | bytes 6291456 | tf_op jit(solution)/shard_map/convert_element_type | solution.py:92
  386.8 5.7 %reshape.225 = bf16[12,256,512]{2,1,0:T(8,128)(2,1)} reshape(bf16[3072,4,128]{2,1,0:T(4,128)(2,1)} %copy.142) | data formatting | bytes 6291456 | tf_op jit(solution)/shard_map/reshape | solution.py:96
  426.7 11.8 %fusion.8 = f32[8,128]{1,0:T(8,128)S(1)} fusion(bf16[8,3072,512]{1,2,0:T(8,128)(2,1)} %constant_dynamic-update-slice_fusion, bf16[128,3072,1]{0,1,2:T(8,128)(2,1)S(1)} %bitcast.219, f32[128,512]{0,1:T(8,128)S(1)} %copy.154), kind=kOutput, calls=%fused_computation.33 | convolution fusion | flops 3222273024 | bytes 26218496 | tf_op jit(solution)/shard_map/tf,qfd->qtd/dot_general | solution.py:104
  438.7 40.8 %psum.7 = f32[8,8]{1,0:T(8,128)S(1)} all-reduce(f32[8,8]{1,0:T(8,128)S(1)} %fusion.16), channel_id=1, replica_groups=mesh['dp'=16,'owner'=2] {'dp','owner'}, use_global_device_ids=true, to_apply=%region_4.5 | all-reduce | flops 64 | bytes 512 | tf_op jit(solution)/shard_map/psum | solution.py:139
  (110 shorter events, 144.5 us)
Async XLA Ops:
  0.0 18.8 %copy-start = (bf16[12,256,256]{2,1,0:T(8,128)(2,1)S(1)}, bf16[12,256,256]{2,1,0:T(8,128)(2,1)}, u32[]{:S(2)}) copy-start(bf16[12,256,256]{2,1,0:T(8,128)(2,1)} %param.12) | copy-start | bytes 4718596
  2.1 16.3 %collective-permute-start = (bf16[16,6,256]{2,1,0:T(8,128)(2,1)S(1)}, bf16[16,6,256]{2,1,0:T(8,128)(2,1)S(1)}, u32[]{:S(2)}, u32[]{:S(2)}) collective-permute-start(bf16[16,6,256]{2,1,0:T(8,128)(2,1)S(1)} %fusion.12), channel_id=1, source_target_pairs={{0,1},{1,0},{2,3},{3,2},{4,5},{5,4},{6,7},{7,6},{8,9},{9,8},{10,11... | collective-permute-start | bytes 147464 | tf_op jit(solution)/shard_map/ppermute | solution.py:16
  2.6 107.8 %all-to-all-start = ((bf16[8,16,512]{2,0,1:T(8,128)(2,1)}), bf16[8,16,512]{2,0,1:T(8,128)(2,1)S(1)}, u32[]{:S(2)}, u32[]{:S(2)}) async-start(bf16[8,16,512]{2,0,1:T(8,128)(2,1)} %bitcast.224), calls=%async_computation | async-start | bytes 262144 | tf_op jit(solution)/shard_map/all_to_all | solution.py:121
  64.9 49.9 %copy-start.7 = (bf16[4,128,128]{2,1,0:T(8,128)(2,1)S(1)}, bf16[4,128,128]{2,1,0:T(8,128)(2,1)}, u32[]{:S(2)}) copy-start(bf16[4,128,128]{2,1,0:T(8,128)(2,1)} %param.13) | copy-start | bytes 393220
  110.4 295.2 %all-to-all-start.1 = ((bf16[8,16,512]{2,0,1:T(8,128)(2,1)}), bf16[8,16,512]{2,0,1:T(8,128)(2,1)S(1)}, u32[]{:S(2)}, u32[]{:S(2)}) async-start(bf16[8,16,512]{2,0,1:T(8,128)(2,1)} %bitcast.49), calls=%async_computation.1 | async-start | bytes 262144 | tf_op jit(solution)/shard_map/all_to_all | solution.py:122
  146.0 4.8 copy-start.13
  181.8 4.7 copy-start.12
  217.7 4.7 copy-start.11
  253.5 4.7 copy-start.10
  289.7 4.7 copy-start.9
  325.4 4.7 copy-start.8
  405.7 3.9 copy-start.1
  409.7 3.0 copy-start.2
  412.7 3.0 copy-start.3
  415.7 3.0 copy-start.4
  418.7 3.0 copy-start.5
  421.8 3.0 copy-start.6
  426.7 11.8 %copy-start.14 = (s32[128]{0:T(128)S(1)}, s32[128]{0:T(128)}, u32[]{:S(2)}) copy-start(s32[128]{0:T(128)} %and_select_fusion) | copy-start | bytes 1540
where the time goes:
time: 485 us; the launch traced here: 480 us
  local copies, waits for them, and re-layouts  247 us (51%)
  blocking collectives  127 us (26%)
  matrix products  89.9 us (19%)
  starting transfers between devices  12.8 us (3%)
    convert_element_type x8, local copies, waits for them, and re-layouts, condition(): half_back = jnp.einsum('fnb,ncb->fnc', damped.reshape(-1, in_blocks, in_w...  127 us
    reshape x8, local copies, waits for them, and re-layouts, condition(): half_back.reshape(capacity, block_width, -1)  45.9 us
    all_gather x1, blocking collectives, local(): query_all = lax.all_gather(query_rot, 'dp', axis=0, tiled=True)  45.7 us
    psum x1, blocking collectives, local(): scores = lax.psum(partial_scores, ('dp', 'owner'))  40.8 us
    all_gather x1, blocking collectives, local(): piece_slots = lax.all_gather(train_local, 'dp', axis=0, tiled=True)  40.5 us
    another operation x9, local copies, waits for them, and re-layouts, condition(): return jnp.stack(results)  39.5 us
    dot_general x8, matrix products, condition(): jnp.einsum('ckl,cld->ckd', basis_out, half_back.reshape(capacity, block_w...  36.2 us
    dot_general x8, matrix products, condition(): lax.dot_general(left_side, right_side, (((0,), (0,)), ((), ())), preferre...  30.5 us
  transfers between devices with their start and end apart: 3, of which 0 were waited for; matrix products, arithmetic and copies ran while one was open for 63% of the time, Pallas kernels for 0%

commit v1 on v0

v1 whole, which is shorter than its diff:
```python
import functools
import math

import jax
import jax.numpy as jnp
from jax import lax
from jax.experimental import pallas as pl
from jax.experimental.pallas import tpu as pltpu
from jax.sharding import PartitionSpec as P

NQ = 8
ET = 16
DAMPING = 0.1
MESH = pl.DeviceIdType.MESH
F32 = jnp.float32
BF16 = jnp.bfloat16


def flipped(index, mask, bits):
    for k in range(bits):
        if mask >> k & 1:
            index = index + (1 << k) - (2 << k) * (index // (1 << k) % 2)
    return index


def kernel(
    n, m, local_q, example_count, scale,
    map_ref, out_tok, in_tok, basis_out_hbm, basis_in_hbm, eig_hbm,
    scores_ref,
    gathered, cols, basis_out, basis_in, eig, masked, act_t, acc, parts, owner_parts,
    ag_send, ag_recv, core_send, core_recv, a2a_send, a2a_recv, load_sem,
    part_send, part_recv, own_send, own_recv,
):
    d = lax.axis_index("dp")
    o = lax.axis_index("owner")
    bits = n.bit_length() - 1
    partner = flipped(o, 1, 1)
    blocks = out_tok.shape[0]
    width = out_tok.shape[2]
    capacity = basis_out.shape[0]
    in_blocks, in_width = basis_in.shape[0], basis_in.shape[1]
    rows = n * out_tok.shape[1]
    per_device = out_tok.shape[1]
    half = blocks // 2
    own = o % 2 * blocks

    loads = [
        pltpu.make_async_copy(basis_in_hbm, basis_in, load_sem.at[0]),
        pltpu.make_async_copy(basis_out_hbm, basis_out, load_sem.at[1]),
        pltpu.make_async_copy(eig_hbm, eig, load_sem.at[2]),
    ]
    for load in loads:
        load.start()
    gathered[d, pl.ds(own, blocks)] = out_tok[...]
    cols[d] = in_tok[d]

    barrier = pltpu.get_barrier_semaphore()
    for r in range(1, n):
        pl.semaphore_signal(
            barrier, inc=1, device_id={"dp": (d + r) % n, "owner": o}, device_id_type=MESH
        )
    for r in range(1, m):
        pl.semaphore_signal(
            barrier, inc=1, device_id={"dp": d, "owner": (o + r) % m}, device_id_type=MESH
        )
    pl.semaphore_wait(barrier, n - 1 + m - 1)

    def piece(h, mask):
        return gathered.at[flipped(d, mask, bits), pl.ds(own + h * half, half)]

    def far_piece(h, mask):
        return gathered.at[
            flipped(d, mask, bits), pl.ds(blocks - own + h * half, half)
        ]

    def gather_copy(h, mask, k):
        return pltpu.make_async_remote_copy(
            src_ref=piece(h, mask),
            dst_ref=piece(h, mask),
            send_sem=ag_send.at[h, mask ^ (1 << k)],
            recv_sem=ag_recv.at[h, mask ^ (1 << k)],
            device_id={"dp": flipped(d, 1 << k, bits), "owner": o},
            device_id_type=MESH,
        )

    def gather_arrival(h, mask):
        return pltpu.make_async_remote_copy(
            src_ref=piece(h, mask),
            dst_ref=piece(h, mask),
            send_sem=ag_send.at[h, mask],
            recv_sem=ag_recv.at[h, mask],
            device_id={"dp": flipped(d, 1, bits), "owner": o},
            device_id_type=MESH,
        )

    def core_copy(h, mask, ref):
        return pltpu.make_async_remote_copy(
            src_ref=ref,
            dst_ref=ref,
            send_sem=core_send.at[h, mask],
            recv_sem=core_recv.at[h, mask],
            device_id={"dp": d, "owner": partner},
            device_id_type=MESH,
        )

    def column_copy(r):
        return pltpu.make_async_remote_copy(
            src_ref=in_tok.at[(d + r) % n],
            dst_ref=cols.at[d],
            send_sem=a2a_send.at[r],
            recv_sem=a2a_recv.at[r],
            device_id={"dp": (d + r) % n, "owner": o},
            device_id_type=MESH,
        )

    def column_arrival(r):
        source = (d + n - r) % n
        return pltpu.make_async_remote_copy(
            src_ref=in_tok.at[source],
            dst_ref=cols.at[source],
            send_sem=a2a_send.at[r],
            recv_sem=a2a_recv.at[r],
            device_id={"dp": source, "owner": o},
            device_id_type=MESH,
        )

    first = list(range(bits - 1, -1, -1))
    second = first[:-2] + first[-2:][::-1]
    orders = (first, second)
    known = [[0], [0]]
    sent = []

    def prepare():
        for r in range(1, n):
            column_arrival(r).wait_recv()
        loads[0].wait()
        row = lax.broadcasted_iota(jnp.int32, (rows, in_width), 0)
        inside = row % per_device
        token = row // per_device * local_q + inside
        per_query = n * local_q // NQ
        owner_query = jnp.where(inside < local_q, token // per_query, NQ)
        for j in range(in_blocks):
            at = slice(j * in_width, (j + 1) * in_width)
            columns = cols[:, :, at].reshape(rows, in_width)
            turned = jnp.dot(columns, basis_in[j], preferred_element_type=F32)
            act_t[at, :] = turned.T.astype(BF16)
            for q in range(NQ):
                masked[q, :, at] = jnp.where(owner_query == q, turned, 0.0).astype(BF16)

    for step in range(bits):
        for h in range(2):
            k = orders[h][step]
            for mask in known[h]:
                copy = gather_copy(h, mask, k)
                copy.start()
                sent.append(copy)
        if step == 0:
            for h in range(2):
                copy = core_copy(h, 0, piece(h, 0))
                copy.start()
                sent.append(copy)
            for r in range(1, n):
                copy = column_copy(r)
                copy.start()
                sent.append(copy)
        if step == bits - 1:
            prepare()
        for h in range(2):
            k = orders[h][step]
            fresh = [mask ^ (1 << k) for mask in known[h]]
            for mask in fresh:
                gather_arrival(h, mask).wait_recv()
                copy = core_copy(h, mask, piece(h, mask))
                copy.start()
                sent.append(copy)
            known[h] += fresh
    for h in range(2):
        for mask in range(n):
            core_copy(h, mask, far_piece(h, mask)).wait_recv()
    for load in loads[1:]:
        load.wait()

    acc[...] = jnp.zeros_like(acc)
    base = o // 2 * 2 * blocks
    ranks, held = [], []
    count = 0
    for c in range(2 * blocks):
        mine = (map_ref[base + c] == o).astype(jnp.int32)
        held.append(mine)
        ranks.append(count)
        count = count + mine

    def one_slot(s, carry):
        block = 0
        for c in range(2 * blocks):
            block = block + c * held[c] * (ranks[c] == s).astype(jnp.int32)
        tokens = gathered[:, block].reshape(rows, width)
        turned = jnp.dot(tokens, basis_out[s], preferred_element_type=F32)
        turned = jnp.where(s < count, turned, 0.0)
        turned_t = turned.T
        left = turned_t.astype(BF16)
        start = pl.multiple_of(s * width, width)
        weight = 1.0 / (eig[pl.ds(start, width), :] + DAMPING)
        for q in range(NQ):
            moment = jnp.dot(left, masked[q], preferred_element_type=F32)
            damped = (moment * weight).astype(BF16)
            projected = jnp.dot(damped, act_t[...], preferred_element_type=F32)
            acc[q] += jnp.sum((projected * turned_t).reshape(-1, 8, rows), axis=0)
        return carry

    lax.fori_loop(0, capacity, one_slot, 0)

    per_token = jnp.sum(acc[...], axis=1)
    row = lax.broadcasted_iota(jnp.int32, (rows, 128), 0)
    inside = row % per_device
    token = row // per_device * (per_device - local_q) + inside - local_q
    example = lax.broadcasted_iota(jnp.int32, (rows, 128), 1)
    hot = jnp.where((inside >= local_q) & (token // ET == example), 1.0, 0.0)
    mine = jnp.dot(
        per_token, hot, precision=lax.Precision.HIGHEST, preferred_element_type=F32
    )

    parts[d] = mine

    def part_copy(r, source):
        return pltpu.make_async_remote_copy(
            src_ref=parts.at[source],
            dst_ref=parts.at[source],
            send_sem=part_send.at[r],
            recv_sem=part_recv.at[r],
            device_id={"dp": (d + r) % n, "owner": o},
            device_id_type=MESH,
        )

    def owner_copy(r, source):
        return pltpu.make_async_remote_copy(
            src_ref=owner_parts.at[source],
            dst_ref=owner_parts.at[source],
            send_sem=own_send.at[r],
            recv_sem=own_recv.at[r],
            device_id={"dp": d, "owner": (o + r) % m},
            device_id_type=MESH,
        )

    for r in range(1, n):
        copy = part_copy(r, d)
        copy.start()
        sent.append(copy)
    for r in range(1, n):
        part_copy(r, (d + n - r) % n).wait_recv()
    owner_parts[o] = jnp.sum(parts[...], axis=0)
    for r in range(1, m):
        copy = owner_copy(r, o)
        copy.start()
        sent.append(copy)
    for r in range(1, m):
        owner_copy(r, (o + m - r) % m).wait_recv()
    total = jnp.sum(owner_parts[...], axis=0) * scale
    scores_ref[...] = total[:, :example_count]
    for copy in sent:
        copy.wait_send()


def local(query_out, query_in, train_out, train_in, basis_out, basis_in, eigvals, owner_map):
    n = lax.axis_size("dp")
    m = lax.axis_size("owner")
    capacity, width = basis_out.shape[0], basis_out.shape[1]
    local_q = query_out.shape[0]
    per_device = local_q + train_out.shape[0]
    blocks = query_out.shape[1] // width
    units = eigvals.shape[1]
    rows = n * per_device
    example_count = n * train_out.shape[0] // ET
    out_tok = (
        jnp.concatenate([query_out, train_out], 0)
        .reshape(per_device, blocks, width)
        .transpose(1, 0, 2)
    )
    in_tok = (
        jnp.concatenate([query_in, train_in], 0)
        .reshape(per_device, n, units)
        .transpose(1, 0, 2)
    )
    hidden_total = query_out.shape[1] * m
    per_query = n * local_q // NQ
    scale = 1.0 / math.sqrt(per_query * ET * hidden_total * query_in.shape[1])
    vmem = pl.BlockSpec(memory_space=pltpu.VMEM)
    anywhere = pl.BlockSpec(memory_space=pl.ANY)
    dma = pltpu.SemaphoreType.DMA
    return pl.pallas_call(
        functools.partial(kernel, n, m, local_q, example_count, scale),
        out_shape=jax.ShapeDtypeStruct((NQ, example_count), F32),
        in_specs=[
            pl.BlockSpec(memory_space=pltpu.SMEM),
            vmem,
            vmem,
            anywhere,
            anywhere,
            anywhere,
        ],
        out_specs=vmem,
        scratch_shapes=[
            pltpu.VMEM((n, 2 * blocks, per_device, width), BF16),
            pltpu.VMEM((n, per_device, units), BF16),
            pltpu.VMEM(basis_out.shape, BF16),
            pltpu.VMEM(basis_in.shape, BF16),
            pltpu.VMEM(eigvals.shape, F32),
            pltpu.VMEM((NQ, rows, units), BF16),
            pltpu.VMEM((units, rows), BF16),
            pltpu.VMEM((NQ, 8, rows), F32),
            pltpu.VMEM((n, NQ, 128), F32),
            pltpu.VMEM((m, NQ, 128), F32),
            dma((2, n)),
            dma((2, n)),
            dma((2, n)),
            dma((2, n)),
            dma((n,)),
            dma((n,)),
            dma((3,)),
            dma((n,)),
            dma((n,)),
            dma((m,)),
            dma((m,)),
        ],
        compiler_params=pltpu.CompilerParams(
            collective_id=0, has_side_effects=True, vmem_limit_bytes=56 * 2**20
        ),
    )(owner_map, out_tok, in_tok, basis_out, basis_in, eigvals)


def solution(mesh):
    in_specs = (
        P("dp", "owner"),
        P("dp", None),
        P("dp", "owner"),
        P("dp", None),
        P("owner", None, None),
        P("dp", None, None),
        P("owner", "dp"),
        P(),
    )
    return jax.shard_map(local, mesh=mesh, in_specs=in_specs, out_specs=P(), check_vma=False)
```

time: 485 us -> 61.8 us (0.13)
  local copies, waits for them, and re-layouts: 247 us -> 2.61 us
  blocking collectives: 127 us -> 0 us
  matrix products: 89.9 us -> 0 us
  Pallas kernels: 0 us -> 57.1 us
  starting transfers between devices: 12.8 us -> 0 us
    convert_element_type x9 -> x0, local copies, waits for them, and re-layouts: 127 us -> none  [the longest x8 127 us: condition(): half_back = jnp.einsum('fnb,ncb->fnc', damped.reshape(-1, in_blocks, in_w...]
    dot_general x31 -> x0, matrix products: 89.9 us -> none  [the longest x8 36.2 us: condition(): jnp.einsum('ckl,cld->ckd', basis_out, half_back.reshape(capacity, block_w...]
    all_gather x2 -> x0, blocking collectives: 86.2 us -> none  [the longest x1 45.7 us: local(): query_all = lax.all_gather(query_rot, 'dp', axis=0, tiled=True)]
    pallas_call x0 -> x1, Pallas kernels: none -> 57.1 us  [local(): pl.pallas_call(functools.partial(kernel, n, m, local_q, example_count, sc...]
    reshape x9 -> x2, local copies, waits for them, and re-layouts: 46 us -> 1.34 us  [the longest x1 0.72 us: local(): in_tok = jnp.concatenate([query_in, train_in], 0).reshape(per_device, n,...]
    psum x1 -> x0, blocking collectives: 40.8 us -> none  [local(): scores = lax.psum(partial_scores, ('dp', 'owner'))]
    another operation x10 -> x0, local copies, waits for them, and re-layouts: 39.5 us -> none  [the longest x9 39.5 us: condition(): return jnp.stack(results)]
    unnamed x41 -> x1, local copies, waits for them, and re-layouts: 29.5 us -> 1.27 us
  transfers between devices with their start and end apart: 3 -> 0, of which waited for: 0 -> 0; matrix products, arithmetic and copies ran while one was open for 63% -> 0% of each run, Pallas kernels for 0% -> 0%
where the time goes in v1:
time: 61.8 us; the launch traced here: 61.5 us
  Pallas kernels  57.1 us (92%)
  local copies, waits for them, and re-layouts  2.61 us (4%)
  other arithmetic  1.76 us (3%)
    pallas_call x1, Pallas kernels, local(): pl.pallas_call(functools.partial(kernel, n, m, local_q, example_count, sc...  57.1 us
    unnamed x1, local copies, waits for them, and re-layouts  1.27 us

profile of v1, /device:TPU:0, one launch (start us, length us, event | category | flops | bytes accessed | tf_op | source)
XLA Modules:
  0.0 61.5 jit_solution(2446807597259911647)
XLA Ops:
  0.0 1.0 %pad_maximum_fusion = bf16[16,8192]{1,0:T(8,128)(2,1)S(1)} fusion(bf16[8,8192]{1,0:T(8,128)(2,1)} %param.11, bf16[8,8192]{1,0:T(8,128)(2,1)} %param.9), kind=kLoop, calls=%fused_computation.1 | loop fusion | flops 524288 | bytes 524288 | tf_op jit(solution)/shard_map/concatenate | solution.py:280
  1.0 0.7 %copy.15 = bf16[2,16,8,512]{3,2,0,1:T(8,128)(2,1)} copy(bf16[2,16,8,512]{3,2,1,0:T(8,128)(2,1)S(1)} %bitcast.15) | data formatting | bytes 524288 | tf_op jit(solution)/shard_map/reshape | solution.py:281
  1.7 0.8 %pad_maximum_fusion.1 = bf16[16,2048]{1,0:T(8,128)(2,1)S(1)} fusion(bf16[8,2048]{1,0:T(8,128)(2,1)} %param.10, bf16[8,2048]{1,0:T(8,128)(2,1)} %param.8), kind=kLoop, calls=%fused_computation.3 | loop fusion | flops 131072 | bytes 131072 | tf_op jit(solution)/shard_map/concatenate | solution.py:275
  2.5 0.6 %copy.16 = bf16[2,8,8,256]{3,2,0,1:T(8,128)(2,1)} copy(bf16[2,8,8,256]{3,2,1,0:T(8,128)(2,1)S(1)} %bitcast.17) | data formatting | bytes 131072 | tf_op jit(solution)/shard_map/reshape | solution.py:276
  3.1 57.1 %shard_map.82 = f32[8,8]{1,0:T(8,128)} custom-call(s32[16]{0:T(128)} %map_ref.1, bf16[8,16,256]{2,1,0:T(8,128)(2,1)} %bitcast.16, bf16[16,16,512]{2,1,0:T(8,128)(2,1)} %bitcast.14, bf16[12,256,256]{2,1,0:T(8,128)(2,1)} %basis_out_hbm.1, bf16[4,128,128]{2,1,0:T(8,128)(2,1)} %basis_in_hbm.1, f32[3072,512]{1,0:T(8,128)} %eig_hbm.1), custom_call_target="tpu_custom_call" | custom-call | tf_op jit(solution)/shard_map/pallas_call | solution.py:290
  60.2 1.3 %copy.18 = f32[8,8]{1,0:T(8,128)} copy(f32[8,8]{1,0:T(8,128)} %shard_map.82) | data formatting | bytes 512

commit v2 on v1

--- a/solution.py
+++ b/solution.py
@@ -25,9 +25,9 @@
 
 def kernel(
     n, m, local_q, example_count, scale,
-    map_ref, out_tok, in_tok, basis_out_hbm, basis_in_hbm, eig_hbm,
+    map_ref, query_out, train_out, query_in, train_in, basis_out_hbm, basis_in_hbm, eig_hbm,
     scores_ref,
-    gathered, cols, basis_out, basis_in, eig, masked, act_t, acc, parts, owner_parts,
+    gathered, in_tok, cols, basis_out, basis_in, eig, masked, act, acc, parts, owner_parts,
     ag_send, ag_recv, core_send, core_recv, a2a_send, a2a_recv, load_sem,
     part_send, part_recv, own_send, own_recv,
 ):
@@ -35,12 +35,12 @@
     o = lax.axis_index("owner")
     bits = n.bit_length() - 1
     partner = flipped(o, 1, 1)
-    blocks = out_tok.shape[0]
-    width = out_tok.shape[2]
-    capacity = basis_out.shape[0]
+    capacity, width = basis_out.shape[0], basis_out.shape[1]
+    blocks = query_out.shape[1] // width
+    units = eig.shape[1]
     in_blocks, in_width = basis_in.shape[0], basis_in.shape[1]
-    rows = n * out_tok.shape[1]
-    per_device = out_tok.shape[1]
+    per_device = local_q + train_out.shape[0]
+    rows = n * per_device
     half = blocks // 2
     own = o % 2 * blocks
 
@@ -51,9 +51,6 @@
     ]
     for load in loads:
         load.start()
-    gathered[d, pl.ds(own, blocks)] = out_tok[...]
-    cols[d] = in_tok[d]
-
     barrier = pltpu.get_barrier_semaphore()
     for r in range(1, n):
         pl.semaphore_signal(
@@ -63,6 +60,18 @@
         pl.semaphore_signal(
             barrier, inc=1, device_id={"dp": d, "owner": (o + r) % m}, device_id_type=MESH
         )
+
+    def packed(query_ref, train_ref, at):
+        both = (query_ref[:, at].astype(F32), train_ref[:, at].astype(F32))
+        return jnp.concatenate(both, 0).astype(BF16)
+
+    for b in range(blocks):
+        gathered[d, own + b] = packed(
+            query_out, train_out, slice(b * width, (b + 1) * width)
+        )
+    for j in range(n):
+        in_tok[j] = packed(query_in, train_in, slice(j * units, (j + 1) * units))
+    cols[d] = in_tok[d]
     pl.semaphore_wait(barrier, n - 1 + m - 1)
 
     def piece(h, mask):
@@ -127,8 +136,14 @@
     first = list(range(bits - 1, -1, -1))
     second = first[:-2] + first[-2:][::-1]
     orders = (first, second)
-    known = [[0], [0]]
     sent = []
+
+    local_t = per_device - local_q
+    train_rows = n * local_t
+    token = lax.broadcasted_iota(jnp.int32, (train_rows, rows), 0)
+    place = token // local_t * per_device + local_q + token % local_t
+    at_row = lax.broadcasted_iota(jnp.int32, (train_rows, rows), 1)
+    pick = jnp.where(place == at_row, 1.0, 0.0).astype(BF16)
 
     def prepare():
         for r in range(1, n):
@@ -143,37 +158,39 @@
             at = slice(j * in_width, (j + 1) * in_width)
             columns = cols[:, :, at].reshape(rows, in_width)
             turned = jnp.dot(columns, basis_in[j], preferred_element_type=F32)
-            act_t[at, :] = turned.T.astype(BF16)
+            act[:, at] = jnp.dot(
+                pick, turned.astype(BF16), preferred_element_type=F32
+            ).astype(BF16)
             for q in range(NQ):
                 masked[q, :, at] = jnp.where(owner_query == q, turned, 0.0).astype(BF16)
 
-    for step in range(bits):
-        for h in range(2):
-            k = orders[h][step]
-            for mask in known[h]:
-                copy = gather_copy(h, mask, k)
-                copy.start()
-                sent.append(copy)
-        if step == 0:
-            for h in range(2):
-                copy = core_copy(h, 0, piece(h, 0))
-                copy.start()
-                sent.append(copy)
-            for r in range(1, n):
-                copy = column_copy(r)
-                copy.start()
-                sent.append(copy)
-        if step == bits - 1:
-            prepare()
-        for h in range(2):
-            k = orders[h][step]
-            fresh = [mask ^ (1 << k) for mask in known[h]]
-            for mask in fresh:
-                gather_arrival(h, mask).wait_recv()
-                copy = core_copy(h, mask, piece(h, mask))
-                copy.start()
-                sent.append(copy)
-            known[h] += fresh
+    def begin(copy):
+        copy.start()
+        sent.append(copy)
+
+    def arrived_at(h, mask):
+        return max(p for p in range(bits) if mask >> orders[h][p] & 1)
+
+    def pass_on(h, mask, position):
+        for k in orders[h][position:]:
+            begin(gather_copy(h, mask, k))
+        begin(core_copy(h, mask, piece(h, mask)))
+
+    for h in range(2):
+        pass_on(h, 0, 0)
+    for r in range(1, n):
+        begin(column_copy(r))
+    arrivals = [(h, mask) for mask in range(1, n) for h in range(2)]
+    arrivals.sort(key=lambda a: (a[1].bit_count(), arrived_at(*a)))
+    for h, mask in arrivals:
+        if arrived_at(h, mask) < bits - 1:
+            gather_arrival(h, mask).wait_recv()
+            pass_on(h, mask, arrived_at(h, mask) + 1)
+    prepare()
+    for h, mask in arrivals:
+        if arrived_at(h, mask) == bits - 1:
+            gather_arrival(h, mask).wait_recv()
+            pass_on(h, mask, bits)
     for h in range(2):
         for mask in range(n):
             core_copy(h, mask, far_piece(h, mask)).wait_recv()
@@ -190,32 +207,37 @@
         ranks.append(count)
         count = count + mine
 
-    def one_slot(s, carry):
-        block = 0
-        for c in range(2 * blocks):
-            block = block + c * held[c] * (ranks[c] == s).astype(jnp.int32)
-        tokens = gathered[:, block].reshape(rows, width)
-        turned = jnp.dot(tokens, basis_out[s], preferred_element_type=F32)
-        turned = jnp.where(s < count, turned, 0.0)
-        turned_t = turned.T
-        left = turned_t.astype(BF16)
-        start = pl.multiple_of(s * width, width)
-        weight = 1.0 / (eig[pl.ds(start, width), :] + DAMPING)
+    together = next(g for g in (4, 3, 2, 1) if capacity % g == 0)
+
+    def some_slots(s, carry):
+        lefts, rights = [], []
+        for g in range(together):
+            slot = s * together + g
+            block = 0
+            for c in range(2 * blocks):
+                block = block + c * held[c] * (ranks[c] == slot).astype(jnp.int32)
+            tokens = gathered[:, block].reshape(rows, width)
+            turned = jnp.dot(tokens, basis_out[slot], preferred_element_type=F32)
+            turned = jnp.where(slot < count, turned, 0.0)
+            turned_t = turned.T
+            lefts.append(turned_t.astype(BF16))
+            rights.append(jnp.dot(pick, turned.astype(BF16), preferred_element_type=F32).astype(BF16))
+        left = jnp.concatenate(lefts, 0)
+        right = jnp.concatenate(rights, 1)
+        start = pl.multiple_of(s * together * width, together * width)
+        weight = 1.0 / (eig[pl.ds(start, together * width), :] + DAMPING)
         for q in range(NQ):
             moment = jnp.dot(left, masked[q], preferred_element_type=F32)
             damped = (moment * weight).astype(BF16)
-            projected = jnp.dot(damped, act_t[...], preferred_element_type=F32)
-            acc[q] += jnp.sum((projected * turned_t).reshape(-1, 8, rows), axis=0)
+            acc[q] += jnp.dot(right, damped, preferred_element_type=F32)
         return carry
 
-    lax.fori_loop(0, capacity, one_slot, 0)
-
-    per_token = jnp.sum(acc[...], axis=1)
-    row = lax.broadcasted_iota(jnp.int32, (rows, 128), 0)
-    inside = row % per_device
-    token = row // per_device * (per_device - local_q) + inside - local_q
-    example = lax.broadcasted_iota(jnp.int32, (rows, 128), 1)
-    hot = jnp.where((inside >= local_q) & (token // ET == example), 1.0, 0.0)
+    lax.fori_loop(0, capacity // together, some_slots, 0)
+
+    per_token = jnp.sum(acc[...] * act[...].astype(F32)[None], axis=2)
+    token = lax.broadcasted_iota(jnp.int32, (train_rows, 128), 0)
+    example = lax.broadcasted_iota(jnp.int32, (train_rows, 128), 1)
+    hot = jnp.where(token // ET == example, 1.0, 0.0)
     mine = jnp.dot(
         per_token, hot, precision=lax.Precision.HIGHEST, preferred_element_type=F32
     )
@@ -271,16 +293,6 @@
     units = eigvals.shape[1]
     rows = n * per_device
     example_count = n * train_out.shape[0] // ET
-    out_tok = (
-        jnp.concatenate([query_out, train_out], 0)
-        .reshape(per_device, blocks, width)
-        .transpose(1, 0, 2)
-    )
-    in_tok = (
-        jnp.concatenate([query_in, train_in], 0)
-        .reshape(per_device, n, units)
-        .transpose(1, 0, 2)
-    )
     hidden_total = query_out.shape[1] * m
     per_query = n * local_q // NQ
     scale = 1.0 / math.sqrt(per_query * ET * hidden_total * query_in.shape[1])
@@ -294,6 +306,8 @@
             pl.BlockSpec(memory_space=pltpu.SMEM),
             vmem,
             vmem,
+            vmem,
+            vmem,
             anywhere,
             anywhere,
             anywhere,
@@ -302,12 +316,13 @@
         scratch_shapes=[
             pltpu.VMEM((n, 2 * blocks, per_device, width), BF16),
             pltpu.VMEM((n, per_device, units), BF16),
+            pltpu.VMEM((n, per_device, units), BF16),
             pltpu.VMEM(basis_out.shape, BF16),
             pltpu.VMEM(basis_in.shape, BF16),
             pltpu.VMEM(eigvals.shape, F32),
             pltpu.VMEM((NQ, rows, units), BF16),
-            pltpu.VMEM((units, rows), BF16),
-            pltpu.VMEM((NQ, 8, rows), F32),
+            pltpu.VMEM((n * train_out.shape[0], units), BF16),
+            pltpu.VMEM((NQ, n * train_out.shape[0], units), F32),
             pltpu.VMEM((n, NQ, 128), F32),
             pltpu.VMEM((m, NQ, 128), F32),
             dma((2, n)),
@@ -325,7 +340,7 @@
         compiler_params=pltpu.CompilerParams(
             collective_id=0, has_side_effects=True, vmem_limit_bytes=56 * 2**20
         ),
-    )(owner_map, out_tok, in_tok, basis_out, basis_in, eigvals)
+    )(owner_map, query_out, train_out, query_in, train_in, basis_out, basis_in, eigvals)
 
 
 def solution(mesh):

time: 61.8 us -> 46.4 us (0.75)
  Pallas kernels: 57.1 us -> 45 us
  other arithmetic: 1.76 us -> 0 us
  local copies, waits for them, and re-layouts: 2.61 us -> 1.28 us
    pallas_call x1, Pallas kernels: 57.1 us -> 45 us  [local(): pl.pallas_call(functools.partial(kernel, n, m, local_q, example_count, sc...]
    concatenate x2 -> x0, other arithmetic: 1.76 us -> none  [the longest x1 0.98 us: local(): jnp.concatenate([query_in, train_in], 0).reshape(per_device, n, units)]
    reshape x2 -> x0, local copies, waits for them, and re-layouts: 1.34 us -> none  [the longest x1 0.72 us: local(): in_tok = jnp.concatenate([query_in, train_in], 0).reshape(per_device, n,...]
where the time goes in v2:
time: 46.4 us; the launch traced here: 46.2 us
  Pallas kernels  45 us (97%)
  local copies, waits for them, and re-layouts  1.28 us (3%)
    pallas_call x1, Pallas kernels, local(): pl.pallas_call(functools.partial(kernel, n, m, local_q, example_count, sc...  45 us
    unnamed x1, local copies, waits for them, and re-layouts  1.28 us

profile of v2, /device:TPU:0, one launch (start us, length us, event | category | flops | bytes accessed | tf_op | source)
XLA Modules:
  0.0 46.2 jit_solution(4668229156973616530)
XLA Ops:
  0.0 45.0 %shard_map.82 = f32[8,8]{1,0:T(8,128)} custom-call(s32[16]{0:T(128)} %map_ref.1, bf16[8,2048]{1,0:T(8,128)(2,1)} %query_out.1, bf16[8,2048]{1,0:T(8,128)(2,1)} %train_out.1, bf16[8,8192]{1,0:T(8,128)(2,1)} %query_in.1, bf16[8,8192]{1,0:T(8,128)(2,1)} %train_in.1, bf16[12,256,256]{2,1,0:T(8,128)(2,1)} %basis_out_hbm.1, bf16[4,128,128]{2,1,0:T(8,128)(2,1)} %basis_in_hbm.1, ...), custom_call_target="tpu_custom_call" | custom-call | tf_op jit(solution)/shard_map/pallas_call | solution.py:302
  45.0 1.3 %copy.10 = f32[8,8]{1,0:T(8,128)} copy(f32[8,8]{1,0:T(8,128)} %shard_map.82) | data formatting | bytes 512
